TPU v7x, 32 devices: a whole 2x2x4 slice. The times are simulated.
32 devices in a mesh: groups: 2 (over x), member: 8 (over z, y), replica: 2 (over core).
Axes of the slice: x: 2, y: 2, z: 4, core: 2. Of those that a mesh axis runs over, the one named last changes fastest.
Arguments:
- states: bfloat16 [32768, 1536], P(('groups', 'member', 'replica')), parts along dimension 0, may hold values from -6 to 6
- rewards: float32 [32768], P(('groups', 'member', 'replica')), parts along dimension 0, may hold values from -6 to 6
- offsets: int32 [32768], P(('groups', 'member', 'replica')), parts along dimension 0, may hold values from 1 to 4
- blocks: int32 [32, 8], P(('groups', 'member', 'replica')), parts along dimension 0, may hold values from 0 to 15
- counts: int32 [16], P(('groups', 'member')), parts along dimension 0, may hold values from 64 to 1024, as said below
- w_first: bfloat16 [16, 1536, 1024], P(('groups', 'member')), parts along dimension 0, may hold values from -0.15625 to 0.15625
- b_first: bfloat16 [16, 1024], P(('groups', 'member')), parts along dimension 0, may hold values from -3 to 3
- w_value: bfloat16 [16, 1024], P(('groups', 'member')), parts along dimension 0, may hold values from -0.1875 to 0.1875
Outputs:
- grad_w1: bfloat16 [16, 1536, 1024], P(('groups', 'member')), parts along dimension 0
- grad_b1: float32 [16, 1024], P(('groups', 'member')), parts along dimension 0
- grad_w2: float32 [16, 1024], P(('groups', 'member')), parts along dimension 0
- td_error: float32 [32, 8, 64], P(('groups', 'member', 'replica')), parts along dimension 0
There are 2 independent parts, one for each index of `groups`. A program takes and returns all parts, laid end to end along the dimension named above; each array names one. Nothing has to cross between parts.
Inputs may be any that keep to these rules, and one draw needn't show every extreme that they name: `counts`: some member uses all 1024 rows.
All inputs are finite; a program needn't handle non-finite values.
Results may differ from a plain program's by a relative error of at most 0.012.
Values may be sent and summed in bfloat16 or wider, within the bound.
A program may use at most 64 MiB of HBM per device.

v0:
```python
import jax
import jax.numpy as jnp
from jax import lax
from jax.sharding import PartitionSpec as P

PEER_ROWS = 64


discount = 0.8


def silu_slope(pre):
    sigma = jax.nn.sigmoid(pre)
    return sigma * (1.0 + pre * (1.0 - sigma))


def forward_terms(features, reward_rows, offset_rows, mask, weight_one, bias_one, head):
    pre = jnp.dot(features, weight_one, preferred_element_type=jnp.float32) + bias_one
    hidden = jax.nn.silu(pre)
    value = jnp.sum(hidden * head, axis=1).reshape(-1, PEER_ROWS)
    position = jnp.arange(PEER_ROWS, dtype=jnp.int32)
    succ = jnp.minimum(position[None, :] + offset_rows, PEER_ROWS - 1)
    nexts = jnp.take_along_axis(value, succ, axis=1)
    factor = jnp.power(jnp.float32(discount), (succ - position[None, :]).astype(jnp.float32))
    error = (reward_rows + factor * nexts - value).reshape(-1) * mask
    dpre = (-error)[:, None] * head[None, :] * silu_slope(pre)
    part_w2 = jnp.sum((-error)[:, None] * hidden, axis=0)
    return (dpre, error, part_w2)


def per_device(states, rewards, offsets, blocks, counts, w_first, b_first, w_value):
    members_here = lax.axis_size("member")
    runs = states.shape[0] // PEER_ROWS
    width = states.shape[1]
    picks = blocks[0]
    send_states = jnp.take(states.reshape(runs, PEER_ROWS, width), picks, axis=0)
    send_rewards = jnp.take(rewards.reshape(runs, PEER_ROWS), picks, axis=0)
    send_offsets = jnp.take(offsets.reshape(runs, PEER_ROWS), picks, axis=0)
    got_states, got_rewards, got_offsets = (
        lax.all_to_all(send_states, "member", split_axis=0, concat_axis=0, tiled=True),
        lax.all_to_all(
            send_rewards.astype(jnp.bfloat16), "member", split_axis=0, concat_axis=0, tiled=True
        ).astype(send_rewards.dtype),
        lax.all_to_all(send_offsets, "member", split_axis=0, concat_axis=0, tiled=True),
    )
    rows = members_here * PEER_ROWS
    features = got_states.reshape(rows, width)
    replica_index = lax.axis_index("replica")
    order = replica_index * rows + jnp.arange(rows, dtype=jnp.int32)
    mask = (order < counts[0]).astype(jnp.float32)
    weight_one = w_first[0]
    bias_one = b_first[0].astype(jnp.float32)
    head = w_value[0].astype(jnp.float32)
    dpre, error_all, total_w2 = forward_terms(
        features, got_rewards, got_offsets, mask, weight_one, bias_one, head
    )
    total_w1 = lax.dot_general(
        features,
        dpre.astype(jnp.bfloat16),
        (((0,), (0,)), ((), ())),
        preferred_element_type=jnp.float32,
    )
    total_b1 = jnp.sum(dpre, axis=0)
    error_all = error_all.reshape(members_here, PEER_ROWS)
    summed_w1, grad_bias, grad_head = (
        lax.psum(total_w1.astype(jnp.bfloat16), "replica").astype(jnp.float32),
        lax.psum(total_b1.astype(jnp.bfloat16), "replica").astype(jnp.float32),
        lax.psum(total_w2.astype(jnp.bfloat16), "replica").astype(jnp.float32),
    )
    grad_first = summed_w1.astype(jnp.bfloat16)
    returned = lax.all_to_all(error_all, "member", split_axis=0, concat_axis=0, tiled=True)
    return (grad_first[None], grad_bias[None], grad_head[None], returned[None])


def solution(mesh):
    placed = (
        P(("groups", "member", "replica"), None),
        P(("groups", "member", "replica")),
        P(("groups", "member", "replica")),
        P(("groups", "member", "replica"), None),
        P(("groups", "member")),
        P(("groups", "member"), None, None),
        P(("groups", "member"), None),
        P(("groups", "member"), None),
    )
    return jax.shard_map(
        per_device,
        mesh=mesh,
        in_specs=placed,
        out_specs=(
            P(("groups", "member"), None, None),
            P(("groups", "member"), None),
            P(("groups", "member"), None),
            P(("groups", "member", "replica"), None, None),
        ),
        check_vma=False,
    )
```

profile of v0, /device:TPU:11, one launch (start us, length us, event | category | flops | bytes accessed | tf_op | source)
XLA Modules:
  0.0 121.3 jit_solution(3330234219438686857)
XLA Ops:
  7.2 0.0 copy-start
  7.2 0.8 compare_and_fusion
  8.0 0.8 fusion.9
  8.8 0.8 reshape.255
  9.6 0.6 gather_fusion.1
  10.1 0.1 fusion.8
  10.2 0.6 copy.12
  10.8 5.7 %all-to-all-start.1 = ((bf16[8,1,64]{2,1,0:T(2,128)(2,1)}), bf16[8,1,64]{2,1,0:T(2,128)(2,1)S(1)}, u32[]{:S(2)}, u32[]{:S(2)}) async-start(bf16[8,1,64]{2,1,0:T(2,128)(2,1)} %copy.12), calls=%async_computation.1 | async-start | bytes 8192 | tf_op jit(solution)/shard_map/all_to_all | solution.py:41
  16.5 0.8 reshape.256
  17.3 0.6 gather_fusion.2
  17.8 0.7 bitcast_select_fusion
  18.5 0.0 copy-done
  18.5 1.8 %gather_fusion = bf16[8,64,1536]{2,1,0:T(8,128)(2,1)} fusion(bf16[16,64,1536]{2,1,0:T(8,128)(2,1)S(1)} %bitcast.41, s32[1024]{0:T(1024)S(1)} %pad_clamp_fusion), kind=kCustom, calls=%fused_computation | custom fusion | bytes 3145760 | tf_op jit(solution)/shard_map/jit(_take)/gather | solution.py:36
  20.3 0.3 all-to-all-done.1
  20.6 5.2 %all-to-all-start.2 = ((s32[8,1,64]{2,1,0:T(1,128)}), s32[8,1,64]{2,1,0:T(1,128)S(1)}, u32[]{:S(2)}, u32[]{:S(2)}) async-start(s32[8,1,64]{2,1,0:T(1,128)} %bitcast.8), calls=%async_computation.2 | async-start | bytes 8192 | tf_op jit(solution)/shard_map/all_to_all | solution.py:44
  25.7 2.8 %broadcast_select_fusion = bf16[8,64,1536]{2,1,0:T(8,128)(2,1)} fusion(bf16[8,64,1536]{2,1,0:T(8,128)(2,1)} %gather_fusion, pred[8]{0:T(512)(128)(4,1)S(1)} %compare_and_fusion), kind=kLoop, calls=%fused_computation.13 | loop fusion | flops 786432 | bytes 3145736 | tf_op jit(solution)/shard_map/jit(_take)/select_n | solution.py:36
  28.5 0.0 copy-start.1
  28.5 0.0 copy-start.2
  28.5 1.3 %all-to-all-done.2 = s32[8,1,64]{2,1,0:T(1,128)S(1)} async-done(((s32[8,1,64]{2,1,0:T(1,128)}), s32[8,1,64]{2,1,0:T(1,128)S(1)}, u32[]{:S(2)}, u32[]{:S(2)}) %all-to-all-start.2) | async-done | bytes 2080 | tf_op jit(solution)/shard_map/all_to_all | solution.py:44
  29.8 5.4 %all-to-all-start = ((bf16[8,64,1536]{2,1,0:T(8,128)(2,1)}), bf16[8,64,1536]{2,1,0:T(8,128)(2,1)}, u32[]{:S(2)}, u32[]{:S(2)}) async-start(bf16[8,64,1536]{2,1,0:T(8,128)(2,1)} %broadcast_select_fusion), calls=%async_computation | async-start | bytes 3145728 | tf_op jit(solution)/shard_map/all_to_all | solution.py:40
  35.1 0.0 all-reduce.3.cloned.1.call-start
  35.8 0.0 copy-done.1
  35.8 0.0 copy-done.2
  35.9 0.1 add.179
  35.9 0.1 add.176
  36.0 0.1 reshape.258
  36.1 0.5 broadcast.273
  36.6 0.7 reduce.3
  37.3 0.1 all_to_all.22
  37.4 0.1 reshape.285
  37.4 30.9 %all-to-all-done = bf16[8,64,1536]{2,1,0:T(8,128)(2,1)} async-done(((bf16[8,64,1536]{2,1,0:T(8,128)(2,1)}), bf16[8,64,1536]{2,1,0:T(8,128)(2,1)}, u32[]{:S(2)}, u32[]{:S(2)}) %all-to-all-start) | async-done | bytes 1572896 | tf_op jit(solution)/shard_map/all_to_all | solution.py:40
  68.3 5.8 %multiply_reduce_fusion.1 = (f32[512]{0:T(512)S(1)}, f32[512,1024]{1,0:T(8,128)}) fusion(f32[1024]{0:T(1024)S(1)} %bitcast.47, f32[1024]{0:T(1024)S(1)} %bitcast.44, bf16[512,1536]{1,0:T(8,128)(2,1)} %bitcast.4, bf16[1,1536,1024]{2,1,0:T(8,128)(2,1)} %param.13), kind=kOutput, calls=%fused_computation.10 | convolution fusion | flops 1614282240 | bytes 6825984 | tf_op jit(solution)/shard_map/dot_general | solution.py:18
  74.2 0.1 reshape.257
  74.2 2.6 %gather_fusion.3 = f32[512]{0:T(512)S(1)} fusion(f32[8,64]{1,0:T(8,128)S(1)} %reshape.257, s32[512]{0:T(512)S(1)} %reshape.285), kind=kCustom, calls=%fused_computation.3 | custom fusion | bytes 8192 | tf_op jit(solution)/shard_map/jit(take_along_axis)/gather | solution.py:23
  76.9 6.0 %fusion = bf16[1,1536,1024]{2,1,0:T(8,128)(2,1)} fusion(bf16[512,1536]{1,0:T(8,128)(2,1)} %bitcast.4, f32[512,1024]{1,0:T(8,128)} %get-tuple-element.9, f32[512]{0:T(512)S(1)} %select_negate_fusion, f32[1024]{0:T(1024)S(1)} %bitcast.48, f32[1024]{0:T(1024)S(1)} %bitcast.45), kind=kOutput, calls=%fused_computation.5 | convolution fusion | flops 1617952768 | bytes 6825984 | tf_op jit(solution)/shard_map/dot_general | solution.py:57
  82.9 0.0 all-reduce.3.cloned.1.call-update
  82.9 0.1 reduce_sum.32
  83.0 0.1 gather.31
  83.1 0.6 subtract_select_fusion
  83.7 7.7 %all-to-all-start.3 = ((f32[8,1,64]{2,1,0:T(1,128)}), f32[8,1,64]{2,1,0:T(1,128)S(1)}, u32[]{:S(2)}, u32[]{:S(2)}) async-start(f32[8,1,64]{2,1,0:T(1,128)} %bitcast.15), calls=%async_computation.3 | async-start | bytes 8192 | tf_op jit(solution)/shard_map/all_to_all | solution.py:71
  91.4 3.1 %multiply_reduce_fusion = (bf16[1024]{0:T(1024)(128)(2,1)S(1)}, bf16[1024]{0:T(1024)(128)(2,1)S(1)}) fusion(f32[512]{0:T(512)S(1)} %select_negate_fusion, f32[512,1024]{1,0:T(8,128)} %get-tuple-element.9, f32[1024]{0:T(1024)S(1)} %bitcast.46, f32[1024]{0:T(1024)S(1)} %bitcast.49), kind=kLoop, calls=%fused_computation.8 | loop fusion | flops 7337984 | bytes 2111488 | tf_op jit(solution)/shard_map/reduce_sum | solution.py:27
  94.5 3.5 %all-reduce = (bf16[1,1024]{1,0:T(2,128)(2,1)S(1)}, bf16[1,1024]{1,0:T(2,128)(2,1)S(1)}) all-reduce(bf16[1,1024]{1,0:T(2,128)(2,1)S(1)} %broadcast_in_dim.64, bf16[1,1024]{1,0:T(2,128)(2,1)S(1)} %broadcast_in_dim.66), channel_id=1, replica_groups=mesh['groups'=2,'member'=8,'replica'=2] {'replica'}, use_global_device_ids=true, to_apply=%region_3.4 | all-reduce | flops 2048 | bytes 8192 | tf_op jit(solution)/shard_map/psum | solution.py:67
  98.0 0.6 broadcast_in_dim.65
  98.6 0.6 broadcast_in_dim.67
  99.2 0.0 all-to-all-done.3
  99.2 10.8 %all-reduce.3.cloned.1.call-done = bf16[1,1536,1024]{2,1,0:T(8,128)(2,1)} async-done(((bf16[1,1536,1024]{2,1,0:T(8,128)(2,1)}), bf16[1,1536,1024]{2,1,0:T(8,128)(2,1)}) %all-reduce.3.cloned.1.call-update) | async-done | bytes 3145744 | tf_op jit(solution)/shard_map/psum | solution.py:66
  110.0 3.9 %copy.23 = bf16[1,1536,1024]{2,1,0:T(8,128)(2,1)} copy(bf16[1,1536,1024]{2,1,0:T(8,128)(2,1)} %all-reduce.3.cloned.1.call-done) | data formatting | bytes 6291456
  113.8 0.6 copy.24
  (10 shorter events, 0.1 us)
Async XLA Ops:
  7.2 11.3 %copy-start = (bf16[1024,1536]{1,0:T(8,128)(2,1)S(1)}, bf16[1024,1536]{1,0:T(8,128)(2,1)}, u32[]{:S(2)}) copy-start(bf16[1024,1536]{1,0:T(8,128)(2,1)} %param.8) | copy-start | bytes 9437188
  10.8 9.8 %all-to-all-start.1 = ((bf16[8,1,64]{2,1,0:T(2,128)(2,1)}), bf16[8,1,64]{2,1,0:T(2,128)(2,1)S(1)}, u32[]{:S(2)}, u32[]{:S(2)}) async-start(bf16[8,1,64]{2,1,0:T(2,128)(2,1)} %copy.12), calls=%async_computation.1 | async-start | bytes 8192 | tf_op jit(solution)/shard_map/all_to_all | solution.py:41
  20.6 9.2 %all-to-all-start.2 = ((s32[8,1,64]{2,1,0:T(1,128)}), s32[8,1,64]{2,1,0:T(1,128)S(1)}, u32[]{:S(2)}, u32[]{:S(2)}) async-start(s32[8,1,64]{2,1,0:T(1,128)} %bitcast.8), calls=%async_computation.2 | async-start | bytes 8192 | tf_op jit(solution)/shard_map/all_to_all | solution.py:44
  28.5 7.3 %copy-start.1 = (bf16[1,1024]{1,0:T(2,128)(2,1)S(1)}, bf16[1,1024]{1,0:T(2,128)(2,1)}, u32[]{:S(2)}) copy-start(bf16[1,1024]{1,0:T(2,128)(2,1)} %param.14) | copy-start | bytes 6148
  28.5 7.3 %copy-start.2 = (bf16[1,1024]{1,0:T(2,128)(2,1)S(1)}, bf16[1,1024]{1,0:T(2,128)(2,1)}, u32[]{:S(2)}) copy-start(bf16[1,1024]{1,0:T(2,128)(2,1)} %param.15) | copy-start | bytes 6148
  29.8 38.6 %all-to-all-start = ((bf16[8,64,1536]{2,1,0:T(8,128)(2,1)}), bf16[8,64,1536]{2,1,0:T(8,128)(2,1)}, u32[]{:S(2)}, u32[]{:S(2)}) async-start(bf16[8,64,1536]{2,1,0:T(8,128)(2,1)} %broadcast_select_fusion), calls=%async_computation | async-start | bytes 3145728 | tf_op jit(solution)/shard_map/all_to_all | solution.py:40
  35.1 74.8 %all-reduce.3.cloned.1.call-start = ((), (), s32[]{:S(2)}) async-start(), calls=%async_computation.4 | async-start | bytes 6291456 | tf_op jit(solution)/shard_map/psum | solution.py:66
  83.7 15.5 %all-to-all-start.3 = ((f32[8,1,64]{2,1,0:T(1,128)}), f32[8,1,64]{2,1,0:T(1,128)S(1)}, u32[]{:S(2)}, u32[]{:S(2)}) async-start(f32[8,1,64]{2,1,0:T(1,128)} %bitcast.15), calls=%async_computation.3 | async-start | bytes 8192 | tf_op jit(solution)/shard_map/all_to_all | solution.py:71
Sparse Core Ops, SparseCore 0:
  83.0 26.8 all-reduce.2
where the time goes:
time: 123 us; the launch traced here: 121 us
  waiting for transfers between devices  43.2 us (35%)
  starting transfers between devices  24 us (20%)
  between operations  14.8 us (12%)
  local copies, waits for them, and re-layouts  13.3 us (11%)
  matrix products  11.8 us (10%)
  other arithmetic  10.7 us (9%)
  blocking collectives  3.46 us (3%)
    all_to_all x1, waiting for transfers between devices, per_device(): lax.all_to_all(send_states, 'member', split_axis=0, concat_axis=0, tiled=...  30.9 us
    psum x1, waiting for transfers between devices, per_device(): lax.psum(total_w1.astype(jnp.bfloat16), 'replica').astype(jnp.float32)  10.8 us
    all_to_all x1, starting transfers between devices, per_device(): lax.all_to_all(error_all, 'member', split_axis=0, concat_axis=0, tiled=True)  7.73 us
    dot_general x1, matrix products, per_device(): lax.dot_general(features, dpre.astype(jnp.bfloat16), (((0,), (0,)), ((),...  5.98 us
    dot_general x1, matrix products, forward_terms(): jnp.dot(features, weight_one, preferred_element_type=jnp.float32) + bias_one  5.81 us
    all_to_all x1, starting transfers between devices, per_device(): lax.all_to_all(send_rewards.astype(jnp.bfloat16), 'member', split_axis=0,...  5.72 us
    all_to_all x1, starting transfers between devices, per_device(): lax.all_to_all(send_states, 'member', split_axis=0, concat_axis=0, tiled=...  5.38 us
    all_to_all x1, starting transfers between devices, per_device(): lax.all_to_all(send_offsets, 'member', split_axis=0, concat_axis=0, tiled...  5.17 us
  transfers between devices with their start and end apart: 5, of which 4 were waited for; matrix products, arithmetic and copies ran while one was open for 11% of the time, Pallas kernels for 0%

commit v1 on v0

v1 whole, which is shorter than its diff:
```python
import functools
import math

import jax
import jax.numpy as jnp
from jax import lax
from jax.experimental import pallas as pl
from jax.experimental.pallas import tpu as pltpu
from jax.sharding import PartitionSpec as P

PEER_ROWS = 64
LANES = 128
CHUNK = 256
GROUP = 4 * PEER_ROWS

discount = 0.8


def partner(me, step, n):
    out = jnp.int32(0)
    bit = 1
    while bit < n:
        a = lax.rem(lax.div(me, jnp.int32(bit)), jnp.int32(2))
        b = lax.rem(lax.div(jnp.int32(step), jnp.int32(bit)), jnp.int32(2))
        out = out + (a + b - 2 * a * b) * bit
        bit *= 2
    return out


def kernel(
    n,
    blocks, counts, rewards, offsets, bias, head, states_hbm, w_hbm,
    grad_hbm, grad_b1, grad_w2, td,
    states, w, send, feats, aux_send, aux, err_send, err_recv,
    hid, slo, dpre, errs, acc, out_buf, b1_acc, w2_acc,
    local_sem, x_send, x_recv, f_send, f_recv, a_send, a_recv, g_send, g_recv, e_send, e_recv, out_sem,
):
    me = lax.axis_index("member")
    rep = lax.axis_index("replica")
    width = states_hbm.shape[2]
    hidden_units = w_hbm.shape[1]
    groups = n // 2

    load_states = pltpu.make_async_copy(states_hbm, states, local_sem.at[0])
    load_states.start()
    load_w = pltpu.make_async_copy(w_hbm, w, local_sem.at[1])
    load_w.start()

    barrier = pltpu.get_barrier_semaphore()

    def greet(step, carry):
        pl.semaphore_signal(
            barrier, inc=1, device_id={"member": partner(me, step, n)}, device_id_type=pl.DeviceIdType.MESH
        )
        return carry

    lax.fori_loop(1, n, greet, 0)
    pl.semaphore_signal(barrier, inc=1, device_id={"replica": 1 - rep}, device_id_type=pl.DeviceIdType.MESH)

    def rows_of(slot):
        return pl.ds(pl.multiple_of(slot * PEER_ROWS, PEER_ROWS), PEER_ROWS)

    def x_copy(step):
        return pltpu.make_async_remote_copy(
            src_ref=send.at[rows_of(step)], dst_ref=feats.at[rows_of(2 * step + rep)],
            send_sem=x_send.at[step], recv_sem=x_recv.at[step],
            device_id={"member": partner(me, step, n)}, device_id_type=pl.DeviceIdType.MESH,
        )

    def a_copy(step):
        return pltpu.make_async_remote_copy(
            src_ref=aux_send.at[step], dst_ref=aux.at[2 * step + rep],
            send_sem=a_send.at[step], recv_sem=a_recv.at[step],
            device_id={"member": partner(me, step, n)}, device_id_type=pl.DeviceIdType.MESH,
        )

    def f_copy(step):
        return pltpu.make_async_remote_copy(
            src_ref=feats.at[rows_of(2 * step + rep)], dst_ref=feats.at[rows_of(2 * step + rep)],
            send_sem=f_send.at[step], recv_sem=f_recv.at[step],
            device_id={"replica": 1 - rep}, device_id_type=pl.DeviceIdType.MESH,
        )

    def g_copy(step):
        return pltpu.make_async_remote_copy(
            src_ref=aux.at[2 * step + rep], dst_ref=aux.at[2 * step + rep],
            send_sem=g_send.at[step], recv_sem=g_recv.at[step],
            device_id={"replica": 1 - rep}, device_id_type=pl.DeviceIdType.MESH,
        )

    def e_copy(step, to, slot):
        return pltpu.make_async_remote_copy(
            src_ref=err_send.at[step], dst_ref=err_recv.at[slot],
            send_sem=e_send.at[step], recv_sem=e_recv.at[step],
            device_id={"member": to}, device_id_type=pl.DeviceIdType.MESH,
        )

    def picked_aux(run):
        half = lax.rem(run, jnp.int32(2))
        r = rewards[pl.ds(lax.div(run, jnp.int32(2)), 1), :]
        o = offsets[pl.ds(lax.div(run, jnp.int32(2)), 1), :].astype(jnp.float32)
        odd = jnp.full((1, LANES), half, jnp.int32) == 1
        r_other = pltpu.roll(r, PEER_ROWS, 1)
        o_other = pltpu.roll(o, PEER_ROWS, 1)
        lane = lax.broadcasted_iota(jnp.int32, (1, LANES), 1)
        row = jnp.where(
            lane < PEER_ROWS, jnp.where(odd, r_other, r), jnp.where(odd, o, o_other)
        )
        return jnp.broadcast_to(row, (8, LANES))

    def gather_aux(step, carry):
        run = blocks[0, partner(me, step, n)]
        aux_send[step] = picked_aux(run)
        return carry

    lax.fori_loop(1, n, gather_aux, 0)
    aux[rep] = picked_aux(blocks[0, me])
    load_states.wait()

    def gather(step, carry):
        run = blocks[0, partner(me, step, n)]
        send[rows_of(step), :] = states[run]
        return carry

    lax.fori_loop(1, n, gather, 0)
    feats[rows_of(rep), :] = states[blocks[0, me]]

    pl.semaphore_wait(barrier, n)

    def far_first(i, carry):
        step = lax.rem(i + n // 2, jnp.int32(n))
        x_copy(step).start()
        a_copy(step).start()
        return carry

    lax.fori_loop(0, n // 2, far_first, 0)
    f_copy(0).start()
    g_copy(0).start()
    lax.fori_loop(n // 2 + 1, n, far_first, 0)

    b1_acc[...] = jnp.zeros_like(b1_acc)
    w2_acc[...] = jnp.zeros_like(w2_acc)
    acc[...] = jnp.zeros_like(acc)
    load_w.wait()

    def head_group(g):
        for i in range(2):
            step = 2 * g + i

            def arrive():
                x_copy(step).wait_recv()
                f_copy(step).start()
                a_copy(step).wait_recv()
                g_copy(step).start()

            if i == 0:
                pl.when(g > 0)(arrive)
            else:
                arrive()
        for i in range(2):
            f_copy(2 * g + i).wait_recv()
            g_copy(2 * g + i).wait_recv()
        base = pl.multiple_of(g * GROUP, GROUP)
        x = feats[pl.ds(base, GROUP), :]
        total = jnp.zeros((GROUP, LANES), jnp.float32)
        for c in range(hidden_units // CHUNK):
            cols = slice(c * CHUNK, (c + 1) * CHUNK)
            pre = jnp.dot(x, w[:, cols], preferred_element_type=jnp.float32)
            pre = pre + bias[:, cols].astype(jnp.float32)
            hd = head[:, cols].astype(jnp.float32)
            sig = jax.nn.sigmoid(pre)
            h = pre * sig
            hid[:, cols] = h
            slo[:, cols] = (sig + h * (1.0 - sig)) * hd
            hv = h * hd
            for t in range(CHUNK // LANES):
                total = total + hv[:, t * LANES:(t + 1) * LANES]
        value = jnp.sum(total, axis=1, keepdims=True)
        row = lax.broadcasted_iota(jnp.int32, (PEER_ROWS, LANES), 0)
        lane = lax.broadcasted_iota(jnp.int32, (PEER_ROWS, LANES), 1)
        eye = lane == row
        count = counts[0]
        for i in range(4):
            step = 2 * g + i // 2
            half = i % 2
            a = jnp.broadcast_to(aux[4 * g + i][0:1, :], (PEER_ROWS, LANES))
            v = value[i * PEER_ROWS:(i + 1) * PEER_ROWS]
            v_row = jnp.sum(jnp.where(eye, v, 0.0), axis=0, keepdims=True)
            r_col = jnp.sum(jnp.where(eye, a, 0.0), axis=1, keepdims=True)
            o_col = jnp.sum(jnp.where(lane == row + PEER_ROWS, a, 0.0), axis=1, keepdims=True)
            succ = jnp.minimum(row.astype(jnp.float32) + o_col, PEER_ROWS - 1.0)
            nxt = jnp.sum(jnp.where(lane.astype(jnp.float32) == succ, v_row, 0.0), axis=1, keepdims=True)
            factor = jnp.exp2((succ - row.astype(jnp.float32)) * math.log2(discount))
            delta = r_col + factor * nxt - v
            q = (half * n + partner(me, step, n)) * PEER_ROWS + row
            err = jnp.where(q < count, delta, 0.0)
            errs[i * PEER_ROWS:(i + 1) * PEER_ROWS, :] = err
            e_row = jnp.sum(jnp.where(eye, err, 0.0), axis=0, keepdims=True)

            def give():
                err_send[step] = jnp.broadcast_to(e_row, (8, LANES))

            pl.when(rep == half)(give)
        for i in range(2):
            step = 2 * g + i

            def start_err():
                e_copy(step, partner(me, step, n), me).start()

            if i == 0:
                pl.when(g > 0)(start_err)
            else:
                start_err()
        for t in range(hidden_units // LANES):
            cols = slice(t * LANES, (t + 1) * LANES)
            neg = -errs[...]
            dp = neg * slo[:, cols]
            dpre[:, cols] = dp.astype(jnp.bfloat16)
            b1_acc[:, cols] += jnp.sum(dp.reshape(GROUP // 8, 8, LANES), axis=0)
            gw = neg * hid[:, cols]
            w2_acc[:, cols] += jnp.sum(gw.reshape(GROUP // 8, 8, LANES), axis=0)

    def grad_chunk(g, k):
        base = pl.multiple_of(g * GROUP, GROUP)
        cols = pl.ds(pl.multiple_of(k * CHUNK, CHUNK), CHUNK)
        return lax.dot_general(
            feats[pl.ds(base, GROUP), cols], dpre[...],
            (((0,), (0,)), ((), ())), preferred_element_type=jnp.float32,
        )

    def out_rows(k):
        return pl.ds(pl.multiple_of(k * CHUNK, CHUNK), CHUNK)

    def middle(g, carry):
        head_group(g)

        def add(k, c):
            acc[out_rows(k), :] += grad_chunk(g, k)
            return c

        lax.fori_loop(0, width // CHUNK, add, 0)
        return carry

    lax.fori_loop(0, groups - 1, middle, 0)
    last = jnp.int32(groups - 1)
    head_group(last)

    def out_copy(k):
        return pltpu.make_async_copy(out_buf.at[out_rows(k)], grad_hbm.at[out_rows(k)], out_sem.at[k])

    def finish(k, c):
        out_buf[out_rows(k), :] = (acc[out_rows(k), :] + grad_chunk(last, k)).astype(jnp.bfloat16)
        out_copy(k).start()
        return c

    lax.fori_loop(0, width // CHUNK, finish, 0)
    grad_b1[...] = jnp.sum(b1_acc[...], axis=0, keepdims=True)
    grad_w2[...] = jnp.sum(w2_acc[...], axis=0, keepdims=True)

    def drain(step, carry):
        x_copy(step).wait_send()
        a_copy(step).wait_send()
        e_copy(step, partner(me, step, n), me).wait()
        return carry

    lax.fori_loop(1, n, drain, 0)

    def drain_forward(step, carry):
        f_copy(step).wait_send()
        g_copy(step).wait_send()
        return carry

    lax.fori_loop(0, n, drain_forward, 0)
    err_recv[me] = err_send[0]
    for m in range(n):
        td[m:m + 1, :] = err_recv[m][0:1, :PEER_ROWS]

    def finish_out(k, c):
        out_copy(k).wait()
        return c

    lax.fori_loop(0, width // CHUNK, finish_out, 0)


def per_device(states, rewards, offsets, blocks, counts, w_first, b_first, w_value):
    n = lax.axis_size("member")
    rows, width = states.shape
    units = w_first.shape[2]
    runs = rows // PEER_ROWS
    vmem = pl.BlockSpec(memory_space=pltpu.VMEM)
    smem = pl.BlockSpec(memory_space=pltpu.SMEM)
    hbm = pl.BlockSpec(memory_space=pl.ANY)
    f32, bf16 = jnp.float32, jnp.bfloat16
    dma = pltpu.SemaphoreType.DMA
    grad, b1, w2, td = pl.pallas_call(
        functools.partial(kernel, n),
        out_shape=(
            jax.ShapeDtypeStruct((width, units), bf16),
            jax.ShapeDtypeStruct((1, units), f32),
            jax.ShapeDtypeStruct((1, units), f32),
            jax.ShapeDtypeStruct((n, PEER_ROWS), f32),
        ),
        in_specs=[smem, smem, vmem, vmem, vmem, vmem, hbm, hbm],
        out_specs=(hbm, vmem, vmem, vmem),
        scratch_shapes=[
            pltpu.VMEM((runs, PEER_ROWS, width), bf16),
            pltpu.VMEM((width, units), bf16),
            pltpu.VMEM((n * PEER_ROWS, width), bf16),
            pltpu.VMEM((2 * n * PEER_ROWS, width), bf16),
            pltpu.VMEM((n, 8, LANES), f32),
            pltpu.VMEM((2 * n, 8, LANES), f32),
            pltpu.VMEM((n, 8, LANES), f32),
            pltpu.VMEM((n, 8, LANES), f32),
            pltpu.VMEM((GROUP, units), f32),
            pltpu.VMEM((GROUP, units), f32),
            pltpu.VMEM((GROUP, units), bf16),
            pltpu.VMEM((GROUP, LANES), f32),
            pltpu.VMEM((width, units), f32),
            pltpu.VMEM((width, units), bf16),
            pltpu.VMEM((8, units), f32),
            pltpu.VMEM((8, units), f32),
            dma((2,)),
            dma((n,)), dma((n,)), dma((n,)), dma((n,)), dma((n,)), dma((n,)),
            dma((n,)), dma((n,)), dma((n,)), dma((n,)),
            dma((width // CHUNK,)),
        ],
        compiler_params=pltpu.CompilerParams(
            collective_id=0, has_side_effects=True, vmem_limit_bytes=56 * 1024 * 1024,
        ),
        cost_estimate=pl.CostEstimate(
            flops=8 * n * PEER_ROWS * width * units,
            bytes_accessed=2 * (rows * width + 2 * width * units),
            transcendentals=2 * n * PEER_ROWS * units,
        ),
    )(
        blocks, counts, rewards.reshape(-1, LANES), offsets.reshape(-1, LANES),
        b_first, w_value, states.reshape(runs, PEER_ROWS, width), w_first[0],
    )
    return grad[None], b1, w2, td[None]


def solution(mesh):
    placed = (
        P(("groups", "member", "replica"), None),
        P(("groups", "member", "replica")),
        P(("groups", "member", "replica")),
        P(("groups", "member", "replica"), None),
        P(("groups", "member")),
        P(("groups", "member"), None, None),
        P(("groups", "member"), None),
        P(("groups", "member"), None),
    )
    return jax.shard_map(
        per_device,
        mesh=mesh,
        in_specs=placed,
        out_specs=(
            P(("groups", "member"), None, None),
            P(("groups", "member"), None),
            P(("groups", "member"), None),
            P(("groups", "member", "replica"), None, None),
        ),
        check_vma=False,
    )
```

time: 123 us -> 58.5 us (0.48); the launches traced: 121 us -> 58.4 us
  Pallas kernels: 0 us -> 51.4 us
  waiting for transfers between devices: 43.2 us -> 0 us
  starting transfers between devices: 24 us -> 0 us
  between operations: 14.8 us -> 1.31 us
  matrix products: 11.8 us -> 0 us
  other arithmetic: 10.7 us -> 0 us
  local copies, waits for them, and re-layouts: 13.3 us -> 5.65 us
  blocking collectives: 3.46 us -> 0 us
    pallas_call x0 -> x1, Pallas kernels: none -> 51.4 us  [per_device(): pl.pallas_call(functools.partial(kernel, n), out_shape=(jax.ShapeDtypeStr...]
    all_to_all x4 -> x0, waiting for transfers between devices: 32.4 us -> none  [the longest x1 30.9 us: per_device(): lax.all_to_all(send_states, 'member', split_axis=0, concat_axis=0, tiled=...]
    all_to_all x4 -> x0, starting transfers between devices: 24 us -> none  [the longest x1 7.73 us: per_device(): lax.all_to_all(error_all, 'member', split_axis=0, concat_axis=0, tiled=True)]
    dot_general x2 -> x0, matrix products: 11.8 us -> none  [the longest x1 5.98 us: per_device(): lax.dot_general(features, dpre.astype(jnp.bfloat16), (((0,), (0,)), ((),...]
    psum x1 -> x0, waiting for transfers between devices: 10.8 us -> none  [per_device(): lax.psum(total_w1.astype(jnp.bfloat16), 'replica').astype(jnp.float32)]
    gather x6 -> x0, local copies, waits for them, and re-layouts: 5.69 us -> none  [the longest x3 2.79 us: forward_terms(): nexts = jnp.take_along_axis(value, succ, axis=1)]
    select_n x3 -> x0, other arithmetic: 4.22 us -> none  [the longest x2 3.56 us: per_device(): jnp.take(states.reshape(runs, PEER_ROWS, width), picks, axis=0)]
    psum x1 -> x0, blocking collectives: 3.46 us -> none  [per_device(): lax.psum(total_b1.astype(jnp.bfloat16), 'replica').astype(jnp.float32)]
  transfers between devices with their start and end apart: 5 -> 0, of which waited for: 4 -> 0; matrix products, arithmetic and copies ran while one was open for 11% -> 0% of each run, Pallas kernels for 0% -> 0%
where the time goes in v1:
time: 58.5 us; the launch traced here: 58.4 us
  Pallas kernels  51.4 us (88%)
  local copies, waits for them, and re-layouts  5.65 us (10%)
  between operations  1.31 us (2%)
    pallas_call x1, Pallas kernels, per_device(): pl.pallas_call(functools.partial(kernel, n), out_shape=(jax.ShapeDtypeStr...  51.4 us
    unnamed x10, local copies, waits for them, and re-layouts  5.65 us

profile of v1, /device:TPU:11, one launch (start us, length us, event | category | flops | bytes accessed | tf_op | source)
XLA Modules:
  0.0 58.4 jit_solution(11601173174336974415)
XLA Ops:
  1.3 51.4 %shard_map.111 = (bf16[1536,1024]{1,0:T(8,128)(2,1)}, f32[1,1024]{1,0:T(1,128)}, f32[1,1024]{1,0:T(1,128)}, f32[8,64]{1,0:T(8,128)}) custom-call(s32[1,8]{1,0:T(1,128)} %blocks.1, s32[1]{0:T(128)S(6)} %copy.16.counts, f32[8,128]{1,0:T(8,128)} %bitcast.10, s32[8,128]{1,0:T(8,128)} %bitcast.11, bf16[1,1024]{1,0:T(2,128)(2,1)} %bias.1, bf16[1,1024]{1,0:T(2,128)(2,1)} %head.1, ...), custom_call_target="tpu_custom_call" | custom-call | flops 6442450944 | bytes 9437184 | tf_op jit(solution)/shard_map/pallas_call | solution.py:295
  52.7 0.0 copy-start.2
  52.7 0.0 copy-start.1
  52.7 0.0 copy-start
  52.7 3.9 %copy.17 = bf16[1,1536,1024]{2,1,0:T(8,128)(2,1)} copy(bf16[1,1536,1024]{2,1,0:T(8,128)(2,1)} %bitcast.6) | data formatting | bytes 6291456
  56.6 0.0 copy-done.2
  56.6 0.6 %copy.18 = f32[1,1024]{1,0:T(1,128)} copy(f32[1,1024]{1,0:T(1,128)S(1)} %copy-done.2) | data formatting | bytes 8192
  57.2 0.0 copy-done.1
  57.2 0.6 %copy.19 = f32[1,1024]{1,0:T(1,128)} copy(f32[1,1024]{1,0:T(1,128)S(1)} %copy-done.1) | data formatting | bytes 8192
  57.8 0.0 copy-done
  57.8 0.6 %copy.20 = f32[1,8,64]{2,1,0:T(8,128)} copy(f32[1,8,64]{2,1,0:T(8,128)S(1)} %bitcast.7) | data formatting | bytes 4096
Async XLA Ops:
  52.7 3.9 %copy-start.2 = (f32[1,1024]{1,0:T(1,128)S(1)}, f32[1,1024]{1,0:T(1,128)}, u32[]{:S(2)}) copy-start(f32[1,1024]{1,0:T(1,128)} %get-tuple-element.17) | copy-start | bytes 12292
  52.7 4.5 %copy-start.1 = (f32[1,1024]{1,0:T(1,128)S(1)}, f32[1,1024]{1,0:T(1,128)}, u32[]{:S(2)}) copy-start(f32[1,1024]{1,0:T(1,128)} %get-tuple-element.18) | copy-start | bytes 12292
  52.7 5.1 %copy-start = (f32[8,64]{1,0:T(8,128)S(1)}, f32[8,64]{1,0:T(8,128)}, u32[]{:S(2)}) copy-start(f32[8,64]{1,0:T(8,128)} %get-tuple-element.11) | copy-start | bytes 6148

commit v2 on v1

--- a/solution.py
+++ b/solution.py
@@ -30,10 +30,10 @@
 def kernel(
     n,
     blocks, counts, rewards, offsets, bias, head, states_hbm, w_hbm,
-    grad_hbm, grad_b1, grad_w2, td,
+    acc, last_feats, dpre, b1_acc, w2_acc, td,
     states, w, send, feats, aux_send, aux, err_send, err_recv,
-    hid, slo, dpre, errs, acc, out_buf, b1_acc, w2_acc,
-    local_sem, x_send, x_recv, f_send, f_recv, a_send, a_recv, g_send, g_recv, e_send, e_recv, out_sem,
+    hid, slo, errs,
+    local_sem, x_send, x_recv, f_send, f_recv, a_send, a_recv, g_send, g_recv, e_send, e_recv,
 ):
     me = lax.axis_index("member")
     rep = lax.axis_index("replica")
@@ -130,9 +130,13 @@
     def far_first(i, carry):
         step = lax.rem(i + n // 2, jnp.int32(n))
         x_copy(step).start()
+        return carry
+
+    def aux_first(step, carry):
         a_copy(step).start()
         return carry
 
+    lax.fori_loop(1, n, aux_first, 0)
     lax.fori_loop(0, n // 2, far_first, 0)
     f_copy(0).start()
     g_copy(0).start()
@@ -143,6 +147,18 @@
     acc[...] = jnp.zeros_like(acc)
     load_w.wait()
 
+    def aux_forward(step, carry):
+        a_copy(step).wait_recv()
+        g_copy(step).start()
+        return carry
+
+    def aux_arrive(step, carry):
+        g_copy(step).wait_recv()
+        return carry
+
+    lax.fori_loop(1, n, aux_forward, 0)
+    lax.fori_loop(0, n, aux_arrive, 0)
+
     def head_group(g):
         for i in range(2):
             step = 2 * g + i
@@ -150,8 +166,6 @@
             def arrive():
                 x_copy(step).wait_recv()
                 f_copy(step).start()
-                a_copy(step).wait_recv()
-                g_copy(step).start()
 
             if i == 0:
                 pl.when(g > 0)(arrive)
@@ -159,7 +173,6 @@
                 arrive()
         for i in range(2):
             f_copy(2 * g + i).wait_recv()
-            g_copy(2 * g + i).wait_recv()
         base = pl.multiple_of(g * GROUP, GROUP)
         x = feats[pl.ds(base, GROUP), :]
         total = jnp.zeros((GROUP, LANES), jnp.float32)
@@ -168,7 +181,7 @@
             pre = jnp.dot(x, w[:, cols], preferred_element_type=jnp.float32)
             pre = pre + bias[:, cols].astype(jnp.float32)
             hd = head[:, cols].astype(jnp.float32)
-            sig = jax.nn.sigmoid(pre)
+            sig = 0.5 * jnp.tanh(0.5 * pre) + 0.5
             h = pre * sig
             hid[:, cols] = h
             slo[:, cols] = (sig + h * (1.0 - sig)) * hd
@@ -180,6 +193,7 @@
         lane = lax.broadcasted_iota(jnp.int32, (PEER_ROWS, LANES), 1)
         eye = lane == row
         count = counts[0]
+        e_rows = []
         for i in range(4):
             step = 2 * g + i // 2
             half = i % 2
@@ -195,12 +209,10 @@
             q = (half * n + partner(me, step, n)) * PEER_ROWS + row
             err = jnp.where(q < count, delta, 0.0)
             errs[i * PEER_ROWS:(i + 1) * PEER_ROWS, :] = err
-            e_row = jnp.sum(jnp.where(eye, err, 0.0), axis=0, keepdims=True)
-
-            def give():
-                err_send[step] = jnp.broadcast_to(e_row, (8, LANES))
-
-            pl.when(rep == half)(give)
+            e_rows.append(jnp.sum(jnp.where(eye, err, 0.0), axis=0, keepdims=True))
+        mine = jnp.full((8, LANES), rep, jnp.int32) == 0
+        for i in range(2):
+            err_send[2 * g + i] = jnp.where(mine, e_rows[2 * i], e_rows[2 * i + 1])
         for i in range(2):
             step = 2 * g + i
 
@@ -245,17 +257,7 @@
     last = jnp.int32(groups - 1)
     head_group(last)
 
-    def out_copy(k):
-        return pltpu.make_async_copy(out_buf.at[out_rows(k)], grad_hbm.at[out_rows(k)], out_sem.at[k])
-
-    def finish(k, c):
-        out_buf[out_rows(k), :] = (acc[out_rows(k), :] + grad_chunk(last, k)).astype(jnp.bfloat16)
-        out_copy(k).start()
-        return c
-
-    lax.fori_loop(0, width // CHUNK, finish, 0)
-    grad_b1[...] = jnp.sum(b1_acc[...], axis=0, keepdims=True)
-    grad_w2[...] = jnp.sum(w2_acc[...], axis=0, keepdims=True)
+    last_feats[...] = feats[pl.ds((groups - 1) * GROUP, GROUP), :]
 
     def drain(step, carry):
         x_copy(step).wait_send()
@@ -275,11 +277,34 @@
     for m in range(n):
         td[m:m + 1, :] = err_recv[m][0:1, :PEER_ROWS]
 
+
+def final_kernel(acc, feats, dpre, b1_acc, w2_acc, td_in, grad_hbm, grad_b1, grad_w2, td, out_buf, out_sem):
+    def rows(k):
+        return pl.ds(pl.multiple_of(k * CHUNK, CHUNK), CHUNK)
+
+    def out_copy(k):
+        return pltpu.make_async_copy(out_buf.at[rows(k)], grad_hbm.at[rows(k)], out_sem.at[k])
+
+    steps = acc.shape[0] // CHUNK
+
+    def finish(k, c):
+        part = lax.dot_general(
+            feats[:, rows(k)], dpre[...], (((0,), (0,)), ((), ())), preferred_element_type=jnp.float32
+        )
+        out_buf[rows(k), :] = (acc[rows(k), :] + part).astype(jnp.bfloat16)
+        out_copy(k).start()
+        return c
+
+    lax.fori_loop(0, steps, finish, 0)
+    grad_b1[...] = jnp.sum(b1_acc[...], axis=0, keepdims=True)
+    grad_w2[...] = jnp.sum(w2_acc[...], axis=0, keepdims=True)
+    td[...] = td_in[...]
+
     def finish_out(k, c):
         out_copy(k).wait()
         return c
 
-    lax.fori_loop(0, width // CHUNK, finish_out, 0)
+    lax.fori_loop(0, steps, finish_out, 0)
 
 
 def per_device(states, rewards, offsets, blocks, counts, w_first, b_first, w_value):
@@ -289,19 +314,22 @@
     runs = rows // PEER_ROWS
     vmem = pl.BlockSpec(memory_space=pltpu.VMEM)
     smem = pl.BlockSpec(memory_space=pltpu.SMEM)
-    hbm = pl.BlockSpec(memory_space=pl.ANY)
+    hbm = pl.BlockSpec(memory_space=pltpu.HBM)
     f32, bf16 = jnp.float32, jnp.bfloat16
     dma = pltpu.SemaphoreType.DMA
-    grad, b1, w2, td = pl.pallas_call(
+    limit = 55 * 2**20
+    held = pl.pallas_call(
         functools.partial(kernel, n),
         out_shape=(
-            jax.ShapeDtypeStruct((width, units), bf16),
-            jax.ShapeDtypeStruct((1, units), f32),
-            jax.ShapeDtypeStruct((1, units), f32),
-            jax.ShapeDtypeStruct((n, PEER_ROWS), f32),
+            pltpu.VMEM((width, units), f32),
+            pltpu.VMEM((GROUP, width), bf16),
+            pltpu.VMEM((GROUP, units), bf16),
+            pltpu.VMEM((8, units), f32),
+            pltpu.VMEM((8, units), f32),
+            pltpu.VMEM((n, PEER_ROWS), f32),
         ),
         in_specs=[smem, smem, vmem, vmem, vmem, vmem, hbm, hbm],
-        out_specs=(hbm, vmem, vmem, vmem),
+        out_specs=(vmem,) * 6,
         scratch_shapes=[
             pltpu.VMEM((runs, PEER_ROWS, width), bf16),
             pltpu.VMEM((width, units), bf16),
@@ -313,19 +341,13 @@
             pltpu.VMEM((n, 8, LANES), f32),
             pltpu.VMEM((GROUP, units), f32),
             pltpu.VMEM((GROUP, units), f32),
-            pltpu.VMEM((GROUP, units), bf16),
             pltpu.VMEM((GROUP, LANES), f32),
-            pltpu.VMEM((width, units), f32),
-            pltpu.VMEM((width, units), bf16),
-            pltpu.VMEM((8, units), f32),
-            pltpu.VMEM((8, units), f32),
             dma((2,)),
             dma((n,)), dma((n,)), dma((n,)), dma((n,)), dma((n,)), dma((n,)),
             dma((n,)), dma((n,)), dma((n,)), dma((n,)),
-            dma((width // CHUNK,)),
         ],
         compiler_params=pltpu.CompilerParams(
-            collective_id=0, has_side_effects=True, vmem_limit_bytes=56 * 1024 * 1024,
+            collective_id=0, has_side_effects=True, vmem_limit_bytes=limit,
         ),
         cost_estimate=pl.CostEstimate(
             flops=8 * n * PEER_ROWS * width * units,
@@ -336,6 +358,22 @@
         blocks, counts, rewards.reshape(-1, LANES), offsets.reshape(-1, LANES),
         b_first, w_value, states.reshape(runs, PEER_ROWS, width), w_first[0],
     )
+    grad, b1, w2, td = pl.pallas_call(
+        final_kernel,
+        out_shape=(
+            jax.ShapeDtypeStruct((width, units), bf16),
+            jax.ShapeDtypeStruct((1, units), f32),
+            jax.ShapeDtypeStruct((1, units), f32),
+            jax.ShapeDtypeStruct((n, PEER_ROWS), f32),
+        ),
+        in_specs=[vmem] * 6,
+        out_specs=(hbm, vmem, vmem, vmem),
+        scratch_shapes=[pltpu.VMEM((width, units), bf16), dma((width // CHUNK,))],
+        compiler_params=pltpu.CompilerParams(vmem_limit_bytes=24 * 1024 * 1024),
+        cost_estimate=pl.CostEstimate(
+            flops=2 * GROUP * width * units, bytes_accessed=2 * width * units, transcendentals=0
+        ),
+    )(*held)
     return grad[None], b1, w2, td[None]
 
 

time: 58.5 us -> 54.7 us (0.935)
  the two profiles are of different devices: /device:TPU:11 before, /device:TPU:0 now
where the time goes in v2:
time: 54.7 us; the launch traced here: 54.5 us
  Pallas kernels  53.2 us (97%)
  between operations  1.29 us (2%)
    pallas_call x1, Pallas kernels, per_device(): pl.pallas_call(functools.partial(kernel, n), out_shape=(pltpu.VMEM((width...  49.8 us
    pallas_call x1, Pallas kernels, per_device(): pl.pallas_call(final_kernel, out_shape=(jax.ShapeDtypeStruct((width, unit...  3.44 us

profile of v2, /device:TPU:0, one launch (start us, length us, event | category | flops | bytes accessed | tf_op | source)
XLA Modules:
  0.0 54.5 jit_solution(2192600979321594283)
XLA Ops:
  1.3 49.8 %shard_map.111 = (f32[1536,1024]{1,0:T(8,128)S(1)}, bf16[256,1536]{1,0:T(8,128)(2,1)S(1)}, bf16[256,1024]{1,0:T(8,128)(2,1)S(1)}, f32[8,1024]{1,0:T(8,128)S(1)},...) custom-call(s32[1,8]{1,0:T(1,128)} %blocks.1, s32[1]{0:T(128)S(6)} %copy.12.counts, f32[8,128]{1,0:T(8,128)} %bitcast.9, ...), custom_call_target="tpu_custom_call" | custom-call | flops 6442450944 | bytes 9437184 | tf_op jit(solution)/shard_map/pallas_call | solution.py:321
  51.1 3.4 %shard_map.112 = (bf16[1536,1024]{1,0:T(8,128)(2,1)}, f32[1,1024]{1,0:T(1,128)}, f32[1,1024]{1,0:T(1,128)}, f32[8,64]{1,0:T(8,128)}) custom-call(f32[1536,1024]{1,0:T(8,128)S(1)} %get-tuple-element.14.acc, bf16[256,1536]{1,0:T(8,128)(2,1)S(1)} %get-tuple-element.15.feats, bf16[256,1024]{1,0:T(8,128)(2,1)S(1)} %get-tuple-element.16.dpre, ...), custom_call_target="tpu_custom_call" | custom-call | flops 805306368 | bytes 3145728 | tf_op jit(solution)/shard_map/pallas_call | solution.py:361

commit v3 on v2

--- a/solution.py
+++ b/solution.py
@@ -30,9 +30,9 @@
 def kernel(
     n,
     blocks, counts, rewards, offsets, bias, head, states_hbm, w_hbm,
-    acc, last_feats, dpre, b1_acc, w2_acc, td,
+    grad, b1_acc, w2_acc, td,
     states, w, send, feats, aux_send, aux, err_send, err_recv,
-    hid, slo, errs,
+    hid, slo, errs, acc, dpre,
     local_sem, x_send, x_recv, f_send, f_recv, a_send, a_recv, g_send, g_recv, e_send, e_recv,
 ):
     me = lax.axis_index("member")
@@ -159,7 +159,7 @@
     lax.fori_loop(1, n, aux_forward, 0)
     lax.fori_loop(0, n, aux_arrive, 0)
 
-    def head_group(g):
+    def head_group(g, slot):
         for i in range(2):
             step = 2 * g + i
 
@@ -227,16 +227,16 @@
             cols = slice(t * LANES, (t + 1) * LANES)
             neg = -errs[...]
             dp = neg * slo[:, cols]
-            dpre[:, cols] = dp.astype(jnp.bfloat16)
+            dpre[slot * GROUP:(slot + 1) * GROUP, cols] = dp.astype(jnp.bfloat16)
             b1_acc[:, cols] += jnp.sum(dp.reshape(GROUP // 8, 8, LANES), axis=0)
             gw = neg * hid[:, cols]
             w2_acc[:, cols] += jnp.sum(gw.reshape(GROUP // 8, 8, LANES), axis=0)
 
-    def grad_chunk(g, k):
+    def grad_chunk(g, k, rows):
         base = pl.multiple_of(g * GROUP, GROUP)
         cols = pl.ds(pl.multiple_of(k * CHUNK, CHUNK), CHUNK)
         return lax.dot_general(
-            feats[pl.ds(base, GROUP), cols], dpre[...],
+            feats[pl.ds(base, rows), cols], dpre[:rows, :],
             (((0,), (0,)), ((), ())), preferred_element_type=jnp.float32,
         )
 
@@ -244,20 +244,25 @@
         return pl.ds(pl.multiple_of(k * CHUNK, CHUNK), CHUNK)
 
     def middle(g, carry):
-        head_group(g)
+        head_group(g, 0)
 
         def add(k, c):
-            acc[out_rows(k), :] += grad_chunk(g, k)
+            acc[out_rows(k), :] += grad_chunk(g, k, GROUP)
             return c
 
         lax.fori_loop(0, width // CHUNK, add, 0)
         return carry
 
-    lax.fori_loop(0, groups - 1, middle, 0)
-    last = jnp.int32(groups - 1)
-    head_group(last)
-
-    last_feats[...] = feats[pl.ds((groups - 1) * GROUP, GROUP), :]
+    lax.fori_loop(0, groups - 2, middle, 0)
+    before = jnp.int32(groups - 2)
+    head_group(before, 0)
+    head_group(jnp.int32(groups - 1), 1)
+
+    def finish(k, c):
+        grad[out_rows(k), :] = (acc[out_rows(k), :] + grad_chunk(before, k, 2 * GROUP)).astype(jnp.bfloat16)
+        return c
+
+    lax.fori_loop(0, width // CHUNK, finish, 0)
 
     def drain(step, carry):
         x_copy(step).wait_send()
@@ -278,33 +283,20 @@
         td[m:m + 1, :] = err_recv[m][0:1, :PEER_ROWS]
 
 
-def final_kernel(acc, feats, dpre, b1_acc, w2_acc, td_in, grad_hbm, grad_b1, grad_w2, td, out_buf, out_sem):
-    def rows(k):
-        return pl.ds(pl.multiple_of(k * CHUNK, CHUNK), CHUNK)
+def final_kernel(grad, b1_acc, w2_acc, td_in, grad_hbm, grad_b1, grad_w2, td, out_sem):
+    steps = grad.shape[0] // CHUNK
 
     def out_copy(k):
-        return pltpu.make_async_copy(out_buf.at[rows(k)], grad_hbm.at[rows(k)], out_sem.at[k])
-
-    steps = acc.shape[0] // CHUNK
-
-    def finish(k, c):
-        part = lax.dot_general(
-            feats[:, rows(k)], dpre[...], (((0,), (0,)), ((), ())), preferred_element_type=jnp.float32
-        )
-        out_buf[rows(k), :] = (acc[rows(k), :] + part).astype(jnp.bfloat16)
+        rows = slice(k * CHUNK, (k + 1) * CHUNK)
+        return pltpu.make_async_copy(grad.at[rows], grad_hbm.at[rows], out_sem.at[k])
+
+    for k in range(steps):
         out_copy(k).start()
-        return c
-
-    lax.fori_loop(0, steps, finish, 0)
     grad_b1[...] = jnp.sum(b1_acc[...], axis=0, keepdims=True)
     grad_w2[...] = jnp.sum(w2_acc[...], axis=0, keepdims=True)
     td[...] = td_in[...]
-
-    def finish_out(k, c):
+    for k in range(steps):
         out_copy(k).wait()
-        return c
-
-    lax.fori_loop(0, steps, finish_out, 0)
 
 
 def per_device(states, rewards, offsets, blocks, counts, w_first, b_first, w_value):
@@ -317,19 +309,17 @@
     hbm = pl.BlockSpec(memory_space=pltpu.HBM)
     f32, bf16 = jnp.float32, jnp.bfloat16
     dma = pltpu.SemaphoreType.DMA
-    limit = 55 * 2**20
+    limit = 60 * 2**20
     held = pl.pallas_call(
         functools.partial(kernel, n),
         out_shape=(
-            pltpu.VMEM((width, units), f32),
-            pltpu.VMEM((GROUP, width), bf16),
-            pltpu.VMEM((GROUP, units), bf16),
+            pltpu.VMEM((width, units), bf16),
             pltpu.VMEM((8, units), f32),
             pltpu.VMEM((8, units), f32),
             pltpu.VMEM((n, PEER_ROWS), f32),
         ),
         in_specs=[smem, smem, vmem, vmem, vmem, vmem, hbm, hbm],
-        out_specs=(vmem,) * 6,
+        out_specs=(vmem,) * 4,
         scratch_shapes=[
             pltpu.VMEM((runs, PEER_ROWS, width), bf16),
             pltpu.VMEM((width, units), bf16),
@@ -342,6 +332,8 @@
             pltpu.VMEM((GROUP, units), f32),
             pltpu.VMEM((GROUP, units), f32),
             pltpu.VMEM((GROUP, LANES), f32),
+            pltpu.VMEM((width, units), f32),
+            pltpu.VMEM((2 * GROUP, units), bf16),
             dma((2,)),
             dma((n,)), dma((n,)), dma((n,)), dma((n,)), dma((n,)), dma((n,)),
             dma((n,)), dma((n,)), dma((n,)), dma((n,)),
@@ -366,12 +358,12 @@
             jax.ShapeDtypeStruct((1, units), f32),
             jax.ShapeDtypeStruct((n, PEER_ROWS), f32),
         ),
-        in_specs=[vmem] * 6,
+        in_specs=[vmem] * 4,
         out_specs=(hbm, vmem, vmem, vmem),
-        scratch_shapes=[pltpu.VMEM((width, units), bf16), dma((width // CHUNK,))],
+        scratch_shapes=[dma((width // CHUNK,))],
         compiler_params=pltpu.CompilerParams(vmem_limit_bytes=24 * 1024 * 1024),
         cost_estimate=pl.CostEstimate(
-            flops=2 * GROUP * width * units, bytes_accessed=2 * width * units, transcendentals=0
+            flops=16 * units, bytes_accessed=2 * width * units, transcendentals=0
         ),
     )(*held)
     return grad[None], b1, w2, td[None]

time: 54.7 us -> 51.9 us (0.949)
  the two profiles are of different devices: /device:TPU:0 before, /device:TPU:11 now
where the time goes in v3:
time: 51.9 us; the launch traced here: 51.7 us
  Pallas kernels  50.4 us (97%)
  between operations  1.29 us (2%)
    pallas_call x1, Pallas kernels, per_device(): pl.pallas_call(functools.partial(kernel, n), out_shape=(pltpu.VMEM((width...  48.1 us
    pallas_call x1, Pallas kernels, per_device(): pl.pallas_call(final_kernel, out_shape=(jax.ShapeDtypeStruct((width, unit...  2.31 us

profile of v3, /device:TPU:11, one launch (start us, length us, event | category | flops | bytes accessed | tf_op | source)
XLA Modules:
  0.0 51.7 jit_solution(5092720908017261933)
XLA Ops:
  1.3 48.1 %shard_map.111 = (bf16[1536,1024]{1,0:T(8,128)(2,1)S(1)}, f32[8,1024]{1,0:T(8,128)S(1)}, f32[8,1024]{1,0:T(8,128)S(1)}, f32[8,64]{1,0:T(8,128)S(1)}) custom-call(s32[1,8]{1,0:T(1,128)} %blocks.1, s32[1]{0:T(128)S(6)} %copy.12.counts, f32[8,128]{1,0:T(8,128)} %bitcast.9, s32[8,128]{1,0:T(8,128)} %bitcast.10, bf16[1,1024]{1,0:T(2,128)(2,1)} %bias.1, ...), custom_call_target="tpu_custom_call" | custom-call | flops 6442450944 | bytes 9437184 | tf_op jit(solution)/shard_map/pallas_call | solution.py:313
  49.4 2.3 %shard_map.112 = (bf16[1536,1024]{1,0:T(8,128)(2,1)}, f32[1,1024]{1,0:T(1,128)}, f32[1,1024]{1,0:T(1,128)}, f32[8,64]{1,0:T(8,128)}) custom-call(bf16[1536,1024]{1,0:T(8,128)(2,1)S(1)} %get-tuple-element.12.grad, f32[8,1024]{1,0:T(8,128)S(1)} %get-tuple-element.13.b1_acc, f32[8,1024]{1,0:T(8,128)S(1)} %get-tuple-element.14.w2_acc, ...), custom_call_target="tpu_custom_call" | custom-call | flops 16384 | bytes 3145728 | tf_op jit(solution)/shard_map/pallas_call | solution.py:353

commit v4 on v3

--- a/solution.py
+++ b/solution.py
@@ -127,9 +127,8 @@
 
     pl.semaphore_wait(barrier, n)
 
-    def far_first(i, carry):
-        step = lax.rem(i + n // 2, jnp.int32(n))
-        x_copy(step).start()
+    def start_rows(i, carry):
+        x_copy(i).start()
         return carry
 
     def aux_first(step, carry):
@@ -137,10 +136,9 @@
         return carry
 
     lax.fori_loop(1, n, aux_first, 0)
-    lax.fori_loop(0, n // 2, far_first, 0)
     f_copy(0).start()
     g_copy(0).start()
-    lax.fori_loop(n // 2 + 1, n, far_first, 0)
+    lax.fori_loop(1, n, start_rows, 0)
 
     b1_acc[...] = jnp.zeros_like(b1_acc)
     w2_acc[...] = jnp.zeros_like(w2_acc)
@@ -160,6 +158,9 @@
     lax.fori_loop(0, n, aux_arrive, 0)
 
     def head_group(g, slot):
+        base = pl.multiple_of(g * GROUP, GROUP)
+        half_group = GROUP // 2
+        totals = []
         for i in range(2):
             step = 2 * g + i
 
@@ -171,24 +172,24 @@
                 pl.when(g > 0)(arrive)
             else:
                 arrive()
-        for i in range(2):
-            f_copy(2 * g + i).wait_recv()
-        base = pl.multiple_of(g * GROUP, GROUP)
-        x = feats[pl.ds(base, GROUP), :]
-        total = jnp.zeros((GROUP, LANES), jnp.float32)
-        for c in range(hidden_units // CHUNK):
-            cols = slice(c * CHUNK, (c + 1) * CHUNK)
-            pre = jnp.dot(x, w[:, cols], preferred_element_type=jnp.float32)
-            pre = pre + bias[:, cols].astype(jnp.float32)
-            hd = head[:, cols].astype(jnp.float32)
-            sig = 0.5 * jnp.tanh(0.5 * pre) + 0.5
-            h = pre * sig
-            hid[:, cols] = h
-            slo[:, cols] = (sig + h * (1.0 - sig)) * hd
-            hv = h * hd
-            for t in range(CHUNK // LANES):
-                total = total + hv[:, t * LANES:(t + 1) * LANES]
-        value = jnp.sum(total, axis=1, keepdims=True)
+            f_copy(step).wait_recv()
+            here = slice(i * half_group, (i + 1) * half_group)
+            x = feats[pl.ds(base + i * half_group, half_group), :]
+            total = jnp.zeros((half_group, LANES), jnp.float32)
+            for c in range(hidden_units // CHUNK):
+                cols = slice(c * CHUNK, (c + 1) * CHUNK)
+                pre = jnp.dot(x, w[:, cols], preferred_element_type=jnp.float32)
+                pre = pre + bias[:, cols].astype(jnp.float32)
+                hd = head[:, cols].astype(jnp.float32)
+                sig = 0.5 * jnp.tanh(0.5 * pre) + 0.5
+                h = pre * sig
+                hid[here, cols] = h
+                slo[here, cols] = (sig + h * (1.0 - sig)) * hd
+                hv = h * hd
+                for t in range(CHUNK // LANES):
+                    total = total + hv[:, t * LANES:(t + 1) * LANES]
+            totals.append(jnp.sum(total, axis=1, keepdims=True))
+        value = jnp.concatenate(totals, axis=0)
         row = lax.broadcasted_iota(jnp.int32, (PEER_ROWS, LANES), 0)
         lane = lax.broadcasted_iota(jnp.int32, (PEER_ROWS, LANES), 1)
         eye = lane == row

time: 51.9 us -> 51.4 us (level)
  no operation moved by 1% of the time
where the time goes in v4:
time: 51.4 us; the launch traced here: 51.2 us
  Pallas kernels  49.9 us (97%)
  between operations  1.29 us (3%)
    pallas_call x1, Pallas kernels, per_device(): pl.pallas_call(functools.partial(kernel, n), out_shape=(pltpu.VMEM((width...  47.6 us
    pallas_call x1, Pallas kernels, per_device(): pl.pallas_call(final_kernel, out_shape=(jax.ShapeDtypeStruct((width, unit...  2.31 us

profile of v4, /device:TPU:11, one launch (start us, length us, event | category | flops | bytes accessed | tf_op | source)
XLA Modules:
  0.0 51.2 jit_solution(12470764373862068045)
XLA Ops:
  1.3 47.6 %shard_map.111 = (bf16[1536,1024]{1,0:T(8,128)(2,1)S(1)}, f32[8,1024]{1,0:T(8,128)S(1)}, f32[8,1024]{1,0:T(8,128)S(1)}, f32[8,64]{1,0:T(8,128)S(1)}) custom-call(s32[1,8]{1,0:T(1,128)} %blocks.1, s32[1]{0:T(128)S(6)} %copy.12.counts, f32[8,128]{1,0:T(8,128)} %bitcast.9, s32[8,128]{1,0:T(8,128)} %bitcast.10, bf16[1,1024]{1,0:T(2,128)(2,1)} %bias.1, ...), custom_call_target="tpu_custom_call" | custom-call | flops 6442450944 | bytes 9437184 | tf_op jit(solution)/shard_map/pallas_call | solution.py:314
  48.9 2.3 %shard_map.112 = (bf16[1536,1024]{1,0:T(8,128)(2,1)}, f32[1,1024]{1,0:T(1,128)}, f32[1,1024]{1,0:T(1,128)}, f32[8,64]{1,0:T(8,128)}) custom-call(bf16[1536,1024]{1,0:T(8,128)(2,1)S(1)} %get-tuple-element.12.grad, f32[8,1024]{1,0:T(8,128)S(1)} %get-tuple-element.13.b1_acc, f32[8,1024]{1,0:T(8,128)S(1)} %get-tuple-element.14.w2_acc, ...), custom_call_target="tpu_custom_call" | custom-call | flops 16384 | bytes 3145728 | tf_op jit(solution)/shard_map/pallas_call | solution.py:354
